TPU v7x, 32 devices: a whole 2x2x4 slice. The times are simulated.
32 devices in a mesh: parts: 2 (over y), req: 4 (over z), tp: 4 (over x, core).
Axes of the slice: x: 2, y: 2, z: 4, core: 2. Of those that a mesh axis runs over, the one named last changes fastest.
Arguments:
- mixer_in: bfloat16 [8192, 8192], P(('parts', 'req'), 'tp'), parts along dimension 0, may hold values from -6 to 6
- maps_in: bfloat16 [8192, 8, 512], P(('parts', 'req'), 'tp'), parts along dimension 0, may hold values from -6 to 6
- delta_raw: bfloat16 [8192, 128], P(('parts', 'req'), 'tp'), parts along dimension 0, may hold values from -5 to 1.5
- conv_cache: bfloat16 [32, 3, 8192], P(('parts', 'req'), None, 'tp'), parts along dimension 0, may hold values from -6 to 6
- maps_cache: bfloat16 [32, 3, 8, 512], P(('parts', 'req'), None, 'tp'), parts along dimension 0, may hold values from -6 to 6
- conv_weight: bfloat16 [4, 8192], P(None, 'tp'), may hold values from -3 to 3
- maps_weight: bfloat16 [4, 8, 512], P(None, 'tp'), may hold values from -3 to 3
- decay_log: float32 [128], P('tp'), may hold values from -3.5 to 0.7
- skip_gain: float32 [128], P('tp'), may hold values from 0.5 to 2
- state_pool: bfloat16 [512, 128, 4, 256], P(('parts', 'req'), 'tp'), parts along dimension 0, may hold values from -0.59765625 to 0.59765625
- queries: bfloat16 [8192, 32, 128], P(('parts', 'req'), 'tp'), parts along dimension 0, may hold values from -7 to 7
- suffix_keyvals: bfloat16 [8192, 8, 256], P(('parts', 'req'), 'tp'), parts along dimension 0, may hold values from -7 to 7
- page_pool: bfloat16 [512, 64, 8, 256], P(('parts', 'req'), None, 'tp'), parts along dimension 0, may hold values from -6 to 6
- prefix_tokens: int32 [32], P('parts'), parts along dimension 0, may hold values from 1 to 1024, as said below
- page_place: int32 [32, 16], P('parts'), parts along dimension 0, may hold values from 0 to 255, as said below
- state_place: int32 [32, 16], P('parts'), parts along dimension 0, may hold values from 0 to 255, as said below
- store_place: int32 [32, 16], P('parts'), parts along dimension 0, may hold values from 0 to 255, as said below
Outputs:
- mixer_out: bfloat16 [8192, 8192], P(('parts', 'req'), 'tp'), parts along dimension 0
- attention_out: bfloat16 [8192, 32, 128], P(('parts', 'req'), 'tp'), parts along dimension 0
- stored_states: bfloat16 [512, 128, 4, 256], P(('parts', 'req'), 'tp'), parts along dimension 0
There are 2 independent parts, one for each index of `parts`. A program takes and returns all parts, laid end to end along the dimension named above; an argument that names none is the same for every part. Nothing has to cross between parts.
Inputs may be any that keep to these rules, and one draw needn't show every extreme that they name: `prefix_tokens`: tokens of request r already cached. Some request has exactly 1024. `page_place`: row of page_pool holding page j of request r: an index along req times 4 * 16, plus a slot. Every row is named exactly once; of the entries of the 4 requests of one index of req, exactly 16 lie on each index of req. Pages from prefix_tokens on are unused. `state_place`: row of state_pool holding head channels j * 4 to (j + 1) * 4 - 1 of request r's state: an index along req times 4 * 16, plus a slot. Every row is named exactly once; of the entries of the 4 requests of one index of req, exactly 16 lie on each index of req. `store_place`: row of stored_states receiving page j of request r's final state, laid out as in state_place, with the same two properties.
All inputs are finite; a program needn't handle non-finite values.
Results may differ from a plain program's by a relative error of at most 0.0062.
Values may be sent and summed in bfloat16 or wider, within the bound.
No kernel may reach another device: no remote copies, remote signals or barrier semaphores. Data moves between devices by JAX's collectives and lax.ppermute only.
A program may use at most 128 MiB of HBM per device.

v0:
```python
import functools

import jax
import jax.numpy as jnp
from jax import lax
from jax.experimental import pallas as pl
from jax.experimental.pallas import tpu as pltpu
from jax.sharding import PartitionSpec as P

APPENDED_LENGTH = 256
REQUESTS_PER_IDX = 4
VMEM_LIMIT = 48 * 1024 * 1024
SHARES = (6, 7, 8, 9, 10, 11, 16)
PASSED = 8
HIDDEN = (((1,), (1,)), ((), ()))


def params():
    return pltpu.CompilerParams(vmem_limit_bytes=VMEM_LIMIT)


def any_spec():
    return pl.BlockSpec(memory_space=pl.ANY)


def hbm_spec():
    return pl.BlockSpec(memory_space=pltpu.HBM)


def own_entries(place_ref, base, slots, position, row, emit):
    for j in range(place_ref.shape[1]):
        slot = place_ref[row, j] - base
        mine = (slot >= 0) & (slot < slots)

        @pl.when(mine)
        def _(slot=slot, position=position, j=j):
            emit(position, slot)

        position = position + jnp.where(mine, 1, 0)
    return position


def gather_kernel(ends_ref, place_ref, pool_ref, out_ref, staged, in_sem, out_sem):
    slots = pool_ref.shape[0]
    base = ends_ref[0] * slots

    def row_step(offset, position):
        def emit(at, slot):
            pltpu.make_async_copy(pool_ref.at[slot], staged.at[at], in_sem).start()

        row = ends_ref[1] * REQUESTS_PER_IDX + offset
        return own_entries(place_ref, base, slots, position, row, emit)

    lax.fori_loop(0, REQUESTS_PER_IDX, row_step, jnp.int32(0))
    pltpu.make_async_copy(pool_ref.at[pl.ds(0, staged.shape[0])], staged, in_sem).wait()
    forward = pltpu.make_async_copy(staged, out_ref, out_sem)
    forward.start()
    forward.wait()


def gather_for(ends, place, pool, capacity):
    shape = (capacity,) + pool.shape[1:]
    size = 2 * capacity * pool[0].size
    return pl.pallas_call(
        gather_kernel,
        out_shape=pltpu.HBM(shape, pool.dtype),
        grid_spec=pltpu.PrefetchScalarGridSpec(
            num_scalar_prefetch=2,
            grid=(1,),
            in_specs=[hbm_spec()],
            out_specs=hbm_spec(),
            scratch_shapes=[
                pltpu.VMEM(shape, pool.dtype),
                pltpu.SemaphoreType.DMA,
                pltpu.SemaphoreType.DMA,
            ],
        ),
        cost_estimate=pl.CostEstimate(flops=0, bytes_accessed=2 * size, transcendentals=0),
        compiler_params=params(),
        name="gather_states",
    )(ends, place, pltpu.with_memory_space_constraint(pool, pltpu.HBM))


def scatter_kernel(ends_ref, place_ref, got_ref, *rest):
    out_ref, staged, in_sem, out_sem = rest[-4:]
    slots = out_ref.shape[0]
    base = ends_ref[0] * slots
    fetch = pltpu.make_async_copy(got_ref, staged, in_sem)
    fetch.start()
    fetch.wait()

    def row_step(offset, position):
        def emit(at, slot):
            pltpu.make_async_copy(staged.at[at], out_ref.at[slot], out_sem).start()

        row = ends_ref[1] * REQUESTS_PER_IDX + offset
        return own_entries(place_ref, base, slots, position, row, emit)

    lax.fori_loop(0, REQUESTS_PER_IDX, row_step, jnp.int32(0))
    pltpu.make_async_copy(staged, out_ref.at[pl.ds(0, staged.shape[0])], out_sem).wait()


def scatter_from(ends, place, got, stored, shape):
    held = [] if stored is None else [stored]
    return pl.pallas_call(
        scatter_kernel,
        out_shape=pltpu.HBM(shape, got.dtype),
        grid_spec=pltpu.PrefetchScalarGridSpec(
            num_scalar_prefetch=2,
            grid=(1,),
            in_specs=[hbm_spec()] * (1 + len(held)),
            out_specs=hbm_spec(),
            scratch_shapes=[
                pltpu.VMEM(got.shape, got.dtype),
                pltpu.SemaphoreType.DMA,
                pltpu.SemaphoreType.DMA,
            ],
        ),
        input_output_aliases={3: 0} if held else {},
        cost_estimate=pl.CostEstimate(
            flops=0, bytes_accessed=4 * got.size, transcendentals=0
        ),
        compiler_params=params(),
        name="scatter_states",
    )(ends, place, got, *held)


def used_entry(place_ref, prefix_ref, page, slots, owner, row, j):
    slot = place_ref[row, j] - owner * slots
    return slot, (slot >= 0) & (slot < slots) & (j * page < prefix_ref[row])


def count_used(place_ref, entry, owner, server):
    def count_row(offset, total):
        for j in range(place_ref.shape[1]):
            _, wanted = entry(owner, server * REQUESTS_PER_IDX + offset, j)
            total = total + jnp.where(wanted, 1, 0)
        return total

    return lax.fori_loop(0, REQUESTS_PER_IDX, count_row, jnp.int32(0))


def partner_of(device):
    return device + 1 - 2 * (device % 2)


def send_kernel(counts, limits_ref, place_ref, prefix_ref, pool_ref, *rest):
    outs, (staged, needs, filled, in_sems, out_sems) = rest[: len(counts)], rest[len(counts) :]
    slots, page = pool_ref.shape[0], pool_ref.shape[2]
    me, limit, choice = limits_ref[0], limits_ref[1], limits_ref[2]
    columns = place_ref.shape[1]
    servers, room = staged.shape[:2]
    entry = functools.partial(used_entry, place_ref, prefix_ref, page, slots)

    def count_server(server, carry):
        needs[server] = count_used(place_ref, entry, me, server)
        return carry

    lax.fori_loop(0, servers, count_server, jnp.int32(0))

    def fetch(slot, server, position):
        return pltpu.make_async_copy(
            pool_ref.at[slot], staged.at[server, position], in_sems.at[server, position]
        )

    def fetch_server(server, carry):
        partner = partner_of(server)
        start = needs[partner] - limit

        def fetch_row(offset, rank):
            for j in range(columns):
                slot, wanted = entry(me, server * REQUESTS_PER_IDX + offset, j)
                wanted = wanted & (server != me)
                direct = rank < limit

                @pl.when(wanted & (direct | (partner != me)))
                def _(slot=slot, rank=rank, direct=direct):
                    fetch(
                        slot,
                        jnp.where(direct, server, partner),
                        jnp.where(direct, rank, start + rank),
                    ).start()

                rank = rank + jnp.where(wanted, 1, 0)
            return rank

        lax.fori_loop(0, REQUESTS_PER_IDX, fetch_row, jnp.int32(0))
        passed = jnp.where(partner == me, 0, jnp.maximum(needs[partner] - limit, 0))
        own = jnp.minimum(needs[server], limit)
        filled[server] = jnp.where(server == me, 0, own + passed)
        return carry

    lax.fori_loop(0, servers, fetch_server, jnp.int32(0))

    def forward(server, option):
        count = counts[option]
        return pltpu.make_async_copy(
            staged.at[server, pl.ds(0, count)],
            outs[option].at[pl.ds(server * count, count)],
            out_sems.at[server],
        )

    def forward_server(server, carry):
        for position in range(room):

            @pl.when(position < filled[server])
            def _(position=position):
                fetch(0, server, position).wait()

        for option in range(len(counts)):

            @pl.when(choice == option)
            def _(option=option):
                forward(server, option).start()

        return carry

    lax.fori_loop(0, servers, forward_server, jnp.int32(0))

    def finish_server(server, carry):
        for option in range(len(counts)):

            @pl.when(choice == option)
            def _(option=option):
                forward(server, option).wait()

        return carry

    lax.fori_loop(0, servers, finish_server, jnp.int32(0))


def send_used(counts, limits, place, prefix, pages):
    servers = lax.axis_size("req")
    shapes = [
        pltpu.HBM((servers * count,) + pages.shape[1:], pages.dtype) for count in counts
    ]
    return pl.pallas_call(
        functools.partial(send_kernel, counts),
        out_shape=shapes,
        grid_spec=pltpu.PrefetchScalarGridSpec(
            num_scalar_prefetch=3,
            grid=(1,),
            in_specs=[any_spec()],
            out_specs=[hbm_spec()] * len(counts),
            scratch_shapes=[
                pltpu.VMEM((servers, counts[-1]) + pages.shape[1:], pages.dtype),
                pltpu.SMEM((servers,), jnp.int32),
                pltpu.SMEM((servers,), jnp.int32),
                pltpu.SemaphoreType.DMA((servers, counts[-1])),
                pltpu.SemaphoreType.DMA((servers,)),
            ],
        ),
        cost_estimate=pl.CostEstimate(
            flops=0, bytes_accessed=2 * pages.size * 2, transcendentals=0
        ),
        compiler_params=params(),
        name="send_used_pages",
    )(limits, place, prefix, pages)


def pass_kernel(counts, limits_ref, place_ref, prefix_ref, pool_ref, *rest):
    gots, (out_ref, staged, in_sems, out_sem) = rest[: len(counts)], rest[len(counts) :]
    slots, page = pool_ref.shape[0], pool_ref.shape[2]
    me, limit, choice = limits_ref[0], limits_ref[1], limits_ref[2]
    columns = place_ref.shape[1]
    servers = place_ref.shape[0] // REQUESTS_PER_IDX
    partner = partner_of(me)
    entry = functools.partial(used_entry, place_ref, prefix_ref, page, slots)

    def fetch(source, index, at):
        return pltpu.make_async_copy(source.at[index], staged.at[at], in_sems.at[at])

    def own_pages(at):
        def row_step(offset, carry):
            rank, at = carry
            for j in range(columns):
                slot, wanted = entry(me, partner * REQUESTS_PER_IDX + offset, j)
                take = wanted & (rank >= limit)

                @pl.when(take)
                def _(slot=slot, at=at):
                    fetch(pool_ref, slot, at).start()

                rank = rank + jnp.where(wanted, 1, 0)
                at = at + jnp.where(take, 1, 0)
            return rank, at

        return lax.fori_loop(0, REQUESTS_PER_IDX, row_step, (jnp.int32(0), at))[1]

    def relayed_pages(owner, at):
        start = count_used(place_ref, entry, owner, me)
        more = jnp.maximum(count_used(place_ref, entry, owner, partner) - limit, 0)

        def page_step(step, carry):
            index = owner * limit + start + step
            for option in range(len(counts)):

                @pl.when(choice == option)
                def _(option=option):
                    fetch(gots[option], index, at + step).start()

            return carry

        lax.fori_loop(0, more, page_step, jnp.int32(0))
        return at + more

    def owner_step(owner, at):
        at = lax.cond(owner == me, own_pages, lambda at: at, at)
        outside = (owner != me) & (owner != partner)
        return lax.cond(outside, lambda at: relayed_pages(owner, at), lambda at: at, at)

    total = lax.fori_loop(0, servers, owner_step, jnp.int32(0))
    for position in range(staged.shape[0]):

        @pl.when(position < total)
        def _(position=position):
            fetch(pool_ref, 0, position).wait()

    forward = pltpu.make_async_copy(staged, out_ref, out_sem)
    forward.start()
    forward.wait()


def pass_on(counts, limits, place, prefix, pages, gots):
    shape = (PASSED,) + pages.shape[1:]
    collected = pl.pallas_call(
        functools.partial(pass_kernel, counts),
        out_shape=pltpu.HBM(shape, pages.dtype),
        grid_spec=pltpu.PrefetchScalarGridSpec(
            num_scalar_prefetch=3,
            grid=(1,),
            in_specs=[any_spec()] * (1 + len(gots)),
            out_specs=hbm_spec(),
            scratch_shapes=[
                pltpu.VMEM(shape, pages.dtype),
                pltpu.SemaphoreType.DMA((PASSED,)),
                pltpu.SemaphoreType.DMA,
            ],
        ),
        cost_estimate=pl.CostEstimate(flops=0, bytes_accessed=2**20, transcendentals=0),
        compiler_params=params(),
        name="pass_pages_on",
    )(limits, place, prefix, pages, *gots)
    swaps = [(peer, peer ^ 1) for peer in range(lax.axis_size("req"))]
    return lax.ppermute(collected, "req", swaps)


def unwritten(shapes):
    return pl.pallas_call(
        lambda *refs: None,
        out_shape=shapes,
        out_specs=[hbm_spec()] * len(shapes),
        cost_estimate=pl.CostEstimate(flops=0, bytes_accessed=0, transcendentals=0),
        name="unwritten",
    )()


def conv_silu(buffer, cache_ref, values, weight_ref):
    length = values.shape[0]
    taps = weight_ref.shape[-2]
    buffer[0:8, :] = cache_ref[...]
    buffer[8:, :] = values.astype(jnp.float32)
    start = 8 - (taps - 1)
    summed = weight_ref[0:1, :] * buffer[start : start + length, :]
    for tap in range(1, taps):
        at = start + tap
        summed = summed + weight_ref[tap : tap + 1, :] * buffer[at : at + length, :]
    return jax.nn.silu(summed).astype(jnp.bfloat16)


def inner_kernel(
    heads,
    x_ref,
    x_cache_ref,
    x_weight_ref,
    maps_ref,
    maps_cache_ref,
    maps_weight_ref,
    decay_row_ref,
    decay_col_ref,
    delta_row_ref,
    tail_ref,
    skip_ref,
    partial_ref,
    update_ref,
    output_map_ref,
    x_buffer,
    maps_buffer,
    x_values,
    scaled,
):
    length, width = x_ref.shape
    head_dim = width // heads
    state = maps_ref.shape[1] // 2
    x_values[...] = conv_silu(x_buffer, x_cache_ref, x_ref[...], x_weight_ref)
    maps = conv_silu(maps_buffer, maps_cache_ref, maps_ref[...], maps_weight_ref)
    input_map, output_map = maps[:, :state], maps[:, state:]
    output_map_ref[...] = output_map
    intersection = lax.dot_general(
        output_map, input_map, HIDDEN, preferred_element_type=jnp.float32
    )
    rows = lax.broadcasted_iota(jnp.int32, (length, length), 0)
    columns = lax.broadcasted_iota(jnp.int32, (length, length), 1)
    causal = rows >= columns
    for h in range(heads):
        lanes = slice(h * head_dim, (h + 1) * head_dim)
        gap = decay_col_ref[:, h : h + 1] - decay_row_ref[h : h + 1, :]
        decays = jnp.where(causal, jnp.exp(jnp.where(causal, gap, 0.0)), 0.0)
        mixing = (intersection * decays * delta_row_ref[h : h + 1, :]).astype(jnp.bfloat16)
        x_head = x_values[:, lanes]
        x_wide = x_head.astype(jnp.float32)
        within = jnp.dot(mixing, x_head, preferred_element_type=jnp.float32)
        partial_ref[:, lanes] = within + skip_ref[:, lanes] * x_wide
        scaled[:, lanes] = (x_wide * tail_ref[:, h : h + 1]).astype(jnp.bfloat16)
    update_ref[...] = lax.dot_general(
        scaled[...], input_map, (((0,), (0,)), ((), ())), preferred_element_type=jnp.float32
    )


def state_kernel(me_ref, state_place_ref, store_place_ref, update_ref, decay_row_ref, *rest):
    peers = (len(rest) - 10) // 2
    gots, prior_ref, sends = rest[:peers], rest[peers], rest[peers + 1 : 2 * peers + 1]
    pages, finals, from_kind, from_index, to_kind, to_index, counts, in_sems, out_sems = rest[
        2 * peers + 1 :
    ]
    request, group = pl.program_id(0), pl.program_id(1)
    page_count, heads, page_rows, state = pages.shape
    slots = gots[0].shape[0]
    head_dim = page_count * page_rows
    joint = 16 // page_rows
    me = me_ref[0]

    @pl.when((request == 0) & (group == 0))
    def _():
        for peer in range(2 * peers):
            counts[peer] = 0

        def row_step(offset, carry):
            for j in range(page_count):
                entry = offset * page_count + j
                place = state_place_ref[me * REQUESTS_PER_IDX + offset, j]
                owner = place // slots
                rank = counts[owner]
                counts[owner] = rank + 1
                distance = (me - owner + peers) % peers
                from_kind[entry] = distance
                from_index[entry] = jnp.where(distance == 0, place - me * slots, rank)
                target = store_place_ref[me * REQUESTS_PER_IDX + offset, j] // slots
                to_index[entry] = counts[peers + target]
                counts[peers + target] = to_index[entry] + 1
                to_kind[entry] = (target - me + peers) % peers
            return carry

        lax.fori_loop(0, REQUESTS_PER_IDX, row_step, jnp.int32(0))

    half = pl.ds(group * heads, heads)

    def arrive(j, kind):
        index = from_index[request * page_count + j]
        return pltpu.make_async_copy(gots[kind].at[index, half], pages.at[j], in_sems.at[j])

    def depart(j, kind):
        index = to_index[request * page_count + j]
        return pltpu.make_async_copy(finals.at[j], sends[kind].at[index, half], out_sems.at[j])

    def start_arrival(j):
        for kind in range(peers):

            @pl.when(from_kind[request * page_count + j] == kind)
            def _(kind=kind):
                arrive(j, kind).start()

    def start_departure(j):
        for kind in range(peers):

            @pl.when(to_kind[request * page_count + j] == kind)
            def _(kind=kind):
                depart(j, kind).start()

    def each(start, end, act):
        def step(j, carry):
            act(j)
            return carry

        lax.fori_loop(start, end, step, jnp.int32(0))

    each(0, page_count, start_arrival)
    last = decay_row_ref.shape[1] - 1
    growths = [jnp.exp(decay_row_ref[h : h + 1, last : last + 1]) for h in range(heads)]

    def joint_step(step, carry):
        first = step * joint
        each(first, first + joint, lambda j: arrive(j, 0).wait())
        for h in range(heads):
            rows = pl.ds(pl.multiple_of(h * head_dim + step * 16, 16), 16)
            old = jnp.concatenate(
                [pages[first + i, h].astype(jnp.float32) for i in range(joint)], axis=0
            )
            prior_ref[rows, :] = old.astype(jnp.bfloat16)
            new = growths[h] * old + update_ref[rows, :]
            for i in range(joint):
                finals[first + i, h] = new[i * page_rows : (i + 1) * page_rows].astype(
                    jnp.bfloat16
                )
        each(first, first + joint, start_departure)
        return carry

    lax.fori_loop(0, page_count // joint, joint_step, jnp.int32(0))
    each(0, page_count, lambda j: depart(j, 0).wait())


def output_kernel(heads, partial_ref, output_map_ref, growth_ref, prior_ref, out_ref):
    head_dim = out_ref.shape[1] // heads
    carried = lax.dot_general(
        output_map_ref[...], prior_ref[...], HIDDEN, preferred_element_type=jnp.float32
    )
    for h in range(heads):
        lanes = slice(h * head_dim, (h + 1) * head_dim)
        out_ref[:, lanes] = (
            partial_ref[:, lanes] + growth_ref[:, h : h + 1] * carried[:, lanes]
        ).astype(jnp.bfloat16)


def list_pages(
    counts, passed, limits_ref, place_ref, prefix_ref, slots, page, kinds, indices, amounts, sizes, ranks
):
    me, limit, choice = limits_ref[0], limits_ref[1], limits_ref[2]
    page_count = place_ref.shape[1]
    peers = ranks.shape[1]
    start_row = me * REQUESTS_PER_IDX
    for peer in range(peers):
        ranks[0, peer] = 0
    if passed:

        def count_row(offset, carry):
            tokens = prefix_ref[start_row + offset]
            for j in range(page_count):
                owner = place_ref[start_row + offset, j] // slots
                ranks[0, owner] = ranks[0, owner] + jnp.where(j * page < tokens, 1, 0)
            return carry

        lax.fori_loop(0, REQUESTS_PER_IDX, count_row, jnp.int32(0))
        begin = jnp.int32(0)
        for peer in range(peers):
            ranks[1, peer] = begin
            begin = begin + jnp.where(peer == me, 0, jnp.maximum(ranks[0, peer] - limit, 0))
            ranks[0, peer] = 0
    def place_row(offset, carry):
        tokens = prefix_ref[start_row + offset]
        at, size = jnp.int32(0), jnp.int32(0)
        for j in range(page_count):
            place = place_ref[start_row + offset, j]
            owner = place // slots
            rank = ranks[0, owner]
            used = j * page < tokens
            ranks[0, owner] = rank + jnp.where(used, 1, 0)
            here = owner == me
            late = (rank >= limit) & jnp.logical_not(here)
            if passed:
                take = used & late
                kind = jnp.int32(0)
                index = ranks[1, owner] + rank - limit
            else:
                take = used & jnp.logical_not(late)
                kind = jnp.where(here, len(counts), choice)
                index = jnp.where(here, place - me * slots, owner * limit + rank)

            @pl.when(take)
            def _(at=at, kind=kind, index=index):
                kinds[offset * page_count + at] = kind
                indices[offset * page_count + at] = index

            at = at + jnp.where(take, 1, 0)
            size = size + jnp.where(take, jnp.minimum(page, tokens - j * page), 0)
        amounts[offset] = at
        sizes[offset] = size
        return carry

    lax.fori_loop(0, REQUESTS_PER_IDX, place_row, jnp.int32(0))


def score(scale, keys, query):
    return lax.dot_general(keys, query, HIDDEN, preferred_element_type=jnp.float32) * scale


def weigh(values, exponent):
    return lax.dot_general(
        values,
        exponent.astype(jnp.bfloat16),
        (((0,), (0,)), ((), ())),
        preferred_element_type=jnp.float32,
    )


def add_pages(scale, query, size, chunk, cached_kv, stats_ref, sums_ref):
    head_dim = query.shape[1]
    keys_at = lax.broadcasted_iota(jnp.int32, (chunk, query.shape[0]), 0)

    def chunk_step(step, carry):
        start = pl.multiple_of(step * chunk, chunk)
        scores = score(scale, cached_kv[pl.ds(start, chunk), :head_dim], query)
        scores = jnp.where(keys_at < size - start, scores, -jnp.inf)
        old = stats_ref[0:1, :]
        top = jnp.maximum(old, jnp.max(scores, axis=0, keepdims=True))
        fade = jnp.exp(old - top)
        exponent = jnp.exp(scores - top)
        stats_ref[0:1, :] = top
        stats_ref[1:2, :] = stats_ref[1:2, :] * fade + jnp.sum(exponent, axis=0, keepdims=True)
        sums_ref[...] = sums_ref[...] * fade + weigh(
            cached_kv[pl.ds(start, chunk), head_dim:], exponent
        )
        return carry

    lax.fori_loop(0, (size + chunk - 1) // chunk, chunk_step, jnp.int32(0))


def attend_kernel(scale, counts, limits_ref, place_ref, prefix_ref, pool_ref, *rest):
    gots = rest[: len(counts)]
    query_ref, fresh_ref, sums_ref, stats_ref = rest[len(counts) : len(counts) + 4]
    cached_kv, kinds, indices, amounts, sizes, ranks, sems = rest[len(counts) + 4 :]
    request, kv_head = pl.program_id(0), pl.program_id(1)
    per_kv, length, head_dim = query_ref.shape
    slots, page = pool_ref.shape[0], pool_ref.shape[2]
    page_count = place_ref.shape[1]

    @pl.when((request == 0) & (kv_head == 0))
    def _():
        cached_kv[...] = jnp.zeros_like(cached_kv)
        list_pages(
            counts, False, limits_ref, place_ref, prefix_ref, slots, page,
            kinds, indices, amounts, sizes, ranks,
        )

    amount = amounts[request]

    def target(j):
        return cached_kv.at[pl.ds(pl.multiple_of(j * page, page), page)]

    def start_copy(j, carry):
        entry = request * page_count + j
        for kind, source in enumerate(gots + (pool_ref,)):

            @pl.when(kinds[entry] == kind)
            def _(source=source):
                pltpu.make_async_copy(
                    source.at[indices[entry], kv_head], target(j), sems.at[j]
                ).start()

        return carry

    lax.fori_loop(0, amount, start_copy, jnp.int32(0))
    query = query_ref[...].reshape(per_kv * length, head_dim)
    keys_at = lax.broadcasted_iota(jnp.int32, (length, per_kv * length), 0)
    queries_at = lax.broadcasted_iota(jnp.int32, (length, per_kv * length), 1) % length
    scores = score(scale, fresh_ref[:, :head_dim], query)
    scores = jnp.where(keys_at <= queries_at, scores, -jnp.inf)
    top = jnp.max(scores, axis=0, keepdims=True)
    exponent = jnp.exp(scores - top)
    stats_ref[0:1, :] = top
    stats_ref[1:2, :] = jnp.sum(exponent, axis=0, keepdims=True)
    sums_ref[...] = weigh(fresh_ref[:, head_dim:], exponent)

    def wait_copy(j, carry):
        pltpu.make_async_copy(pool_ref.at[0, kv_head], target(j), sems.at[j]).wait()
        return carry

    lax.fori_loop(0, amount, wait_copy, jnp.int32(0))
    add_pages(scale, query, sizes[request], length, cached_kv, stats_ref, sums_ref)


def attend_passed_kernel(
    scale,
    counts,
    slots,
    limits_ref,
    place_ref,
    prefix_ref,
    passed_ref,
    query_ref,
    sums_in_ref,
    stats_in_ref,
    out_ref,
    cached_kv,
    sums_ref,
    stats_ref,
    kinds,
    indices,
    amounts,
    sizes,
    ranks,
    sems,
):
    request, kv_head = pl.program_id(0), pl.program_id(1)
    per_kv, length, head_dim = query_ref.shape
    page = passed_ref.shape[2]
    page_count = place_ref.shape[1]

    @pl.when((request == 0) & (kv_head == 0))
    def _():
        cached_kv[...] = jnp.zeros_like(cached_kv)
        list_pages(
            counts, True, limits_ref, place_ref, prefix_ref, slots, page,
            kinds, indices, amounts, sizes, ranks,
        )

    amount = amounts[request]

    def fetch(j, index):
        target = cached_kv.at[pl.ds(pl.multiple_of(j * page, page), page)]
        return pltpu.make_async_copy(passed_ref.at[index, kv_head], target, sems.at[j])

    def start_copy(j, carry):
        fetch(j, indices[request * page_count + j]).start()
        return carry

    def wait_copy(j, carry):
        fetch(j, 0).wait()
        return carry

    @pl.when(amount == 0)
    def _():
        out_ref[...] = (
            (sums_in_ref[...] / stats_in_ref[1:2, :]).T.astype(jnp.bfloat16).reshape(out_ref.shape)
        )

    @pl.when(amount > 0)
    def _():
        lax.fori_loop(0, amount, start_copy, jnp.int32(0))
        sums_ref[...] = sums_in_ref[...]
        stats_ref[...] = stats_in_ref[...]
        lax.fori_loop(0, amount, wait_copy, jnp.int32(0))
        query = query_ref[...].reshape(per_kv * length, head_dim)
        add_pages(scale, query, sizes[request], length, cached_kv, stats_ref, sums_ref)
        out_ref[...] = (
            (sums_ref[...] / stats_ref[1:2, :]).T.astype(jnp.bfloat16).reshape(out_ref.shape)
        )


def body(
    mixer_in,
    maps_in,
    delta_raw,
    conv_cache,
    maps_cache,
    conv_weight,
    maps_weight,
    decay_log,
    skip_gain,
    state_pool,
    queries,
    suffix_keyvals,
    page_pool,
    prefix_tokens,
    page_place,
    state_place,
    store_place,
):
    peers = lax.axis_size("req")
    me = lax.axis_index("req").astype(jnp.int32).reshape(1)
    requests, length = REQUESTS_PER_IDX, APPENDED_LENGTH
    groups = maps_in.shape[1]
    state = maps_in.shape[2] // 2
    heads = delta_raw.shape[1]
    per_group = heads // groups
    width = mixer_in.shape[1]
    group_width = width // groups
    head_dim = width // heads
    slots, _, page_rows, _ = state_pool.shape
    page_count = state_place.shape[1]
    kv_heads = page_pool.shape[2]
    attend_dim = queries.shape[2]
    per_kv = queries.shape[1] // kv_heads
    page = page_pool.shape[1]
    prefix_pages = page_place.shape[1]
    page_slots = page_pool.shape[0]
    pair_pages = requests * prefix_pages // peers
    taps = conv_weight.shape[0]

    def exchange(pages):
        return lax.all_to_all(pages, "req", split_axis=0, concat_axis=0, tiled=True)

    capacity = requests * page_count // peers
    distances = range(1, peers)

    def send_to(distance, pages):
        return lax.ppermute(
            pages, "req", [(peer, (peer + distance) % peers) for peer in range(peers)]
        )

    def ends(distance):
        return jnp.concatenate([me, (me + distance) % peers])

    state_gots = [state_pool] + [
        send_to(distance, gather_for(ends(distance), state_place, state_pool, capacity))
        for distance in distances
    ]

    counts = tuple(sorted({max(1, pair_pages * share // 16) for share in SHARES}))
    used = jnp.arange(prefix_pages)[None, :] * page < prefix_tokens[:, None]
    holders = page_place // page_slots
    pairs = used[:, :, None] & (holders[:, :, None] == jnp.arange(peers)[None, None, :])
    needs = jnp.sum(pairs.reshape(peers, -1, peers).astype(jnp.int32), axis=1)
    places = jnp.arange(peers)
    both = jnp.sum(needs.reshape(peers // 2, 2, peers), axis=1)
    outside = jnp.arange(peers // 2)[:, None] != places[None, :] // 2
    limit_table = jnp.array(counts, jnp.int32)
    crowded = jnp.max(jnp.where(outside, both, 0)) > 2 * limit_table
    rests = jnp.maximum(needs[None] - limit_table[:, None, None], 0)
    rests = jnp.where(places[:, None] != places[None, :], rests, 0)
    crowded = crowded | (jnp.max(jnp.sum(rests, axis=2), axis=1) > PASSED)
    choice = jnp.sum(crowded.astype(jnp.int32))
    limit = jnp.sum(jnp.where(jnp.arange(len(counts)) == choice, limit_table, 0))
    limits = jnp.stack([me[0], limit, choice])
    pages_by_head = page_pool.transpose(0, 2, 1, 3)
    page_sends = send_used(counts, limits, page_place, prefix_tokens, pages_by_head)

    delta = jax.nn.softplus(delta_raw.T.astype(jnp.float32)).reshape(heads, requests, length)
    log_decay = jnp.cumsum(-delta * jnp.exp(decay_log)[:, None, None], axis=2)
    tail = jnp.exp(log_decay[:, :, -1:] - log_decay) * delta
    growth = jnp.exp(log_decay)

    def by_rows(values):
        return values.reshape(groups, per_group, requests, length).transpose(2, 0, 1, 3)

    def by_columns(values):
        return values.reshape(groups, per_group, requests, length).transpose(2, 0, 3, 1)

    decay_row = by_rows(log_decay)
    maps_split = maps_in.transpose(1, 0, 2)
    empty = 8 - (taps - 1)
    x_cache = jnp.pad(conv_cache.astype(jnp.float32), ((0, 0), (empty, 0), (0, 0)))
    maps_edge = jnp.pad(
        maps_cache.transpose(0, 2, 1, 3).astype(jnp.float32), ((0, 0), (0, 0), (empty, 0), (0, 0))
    )
    row_block = pl.BlockSpec((None, None, per_group, length), lambda r, g: (r, g, 0, 0))
    column_block = pl.BlockSpec((None, None, length, per_group), lambda r, g: (r, g, 0, 0))
    x_block = pl.BlockSpec((length, group_width), lambda r, g: (r, g))
    update_block = pl.BlockSpec((None, None, group_width, state), lambda r, g: (r, g, 0, 0))
    map_block = pl.BlockSpec((None, length, state), lambda r, g: (g, r, 0))
    partial, update, output_map = pl.pallas_call(
        functools.partial(inner_kernel, per_group),
        grid=(requests, groups),
        in_specs=[
            x_block,
            pl.BlockSpec((None, 8, group_width), lambda r, g: (r, 0, g)),
            pl.BlockSpec((taps, group_width), lambda r, g: (0, g)),
            pl.BlockSpec((None, length, 2 * state), lambda r, g: (g, r, 0)),
            pl.BlockSpec((None, None, 8, 2 * state), lambda r, g: (r, g, 0, 0)),
            pl.BlockSpec((None, taps, 2 * state), lambda r, g: (g, 0, 0)),
            row_block,
            column_block,
            row_block,
            column_block,
            pl.BlockSpec((1, group_width), lambda r, g: (0, g)),
        ],
        out_specs=[x_block, update_block, map_block],
        out_shape=[
            jax.ShapeDtypeStruct((requests * length, width), jnp.float32),
            jax.ShapeDtypeStruct((requests, groups, group_width, state), jnp.float32),
            jax.ShapeDtypeStruct((groups, requests * length, state), jnp.bfloat16),
        ],
        scratch_shapes=[
            pltpu.VMEM((8 + length, group_width), jnp.float32),
            pltpu.VMEM((8 + length, 2 * state), jnp.float32),
            pltpu.VMEM((length, group_width), jnp.bfloat16),
            pltpu.VMEM((length, group_width), jnp.bfloat16),
        ],
        cost_estimate=pl.CostEstimate(
            flops=3 * requests * length * width * state,
            bytes_accessed=32 * 2**20,
            transcendentals=requests * heads * length * length,
        ),
        compiler_params=params(),
        name="mix_new_tokens",
    )(
        mixer_in,
        x_cache,
        conv_weight.astype(jnp.float32),
        maps_split,
        maps_edge,
        maps_weight.transpose(1, 0, 2).astype(jnp.float32),
        decay_row,
        by_columns(log_decay),
        by_rows(delta),
        by_columns(tail),
        jnp.repeat(skip_gain, head_dim).reshape(1, width),
    )
    growth_col = by_columns(growth)
    grouped_queries = queries.reshape(requests, length, kv_heads, per_kv, attend_dim).transpose(
        0, 2, 3, 1, 4
    )
    fresh = suffix_keyvals.transpose(1, 0, 2)

    page_sends, state_gots, partial, update, output_map, growth_col, decay_row = (
        lax.optimization_barrier(
            (page_sends, state_gots, partial, update, output_map, growth_col, decay_row)
        )
    )
    state_block = pl.BlockSpec((None, None, group_width, state), lambda r, g, *_: (r, g, 0, 0))

    def advance(at, sends, state_gots, update, decay_row):
        shapes = [pltpu.HBM(sent.shape, sent.dtype) for sent in sends]
        others = list(unwritten(shapes[:at] + shapes[at + 1 :])) if len(shapes) > 1 else []
        gots = tuple(others[:at] + [exchange(sends[at])] + others[at:])
        prior, *final_sends = pl.pallas_call(
            state_kernel,
            grid_spec=pltpu.PrefetchScalarGridSpec(
                num_scalar_prefetch=3,
                grid=(requests, groups),
                in_specs=[
                    state_block,
                    pl.BlockSpec((None, None, per_group, length), lambda r, g, *_: (r, g, 0, 0)),
                ]
                + [any_spec()] * peers,
                out_specs=[state_block] + [hbm_spec()] * peers,
                scratch_shapes=[
                    pltpu.VMEM((page_count, per_group, page_rows, state), jnp.bfloat16),
                    pltpu.VMEM((page_count, per_group, page_rows, state), jnp.bfloat16),
                    *[pltpu.SMEM((requests * page_count,), jnp.int32)] * 4,
                    pltpu.SMEM((2 * peers,), jnp.int32),
                    pltpu.SemaphoreType.DMA((page_count,)),
                    pltpu.SemaphoreType.DMA((page_count,)),
                ],
            ),
            out_shape=[
                jax.ShapeDtypeStruct(update.shape, jnp.bfloat16),
                *[pltpu.HBM((capacity,) + state_pool.shape[1:], jnp.bfloat16)] * peers,
            ],
            cost_estimate=pl.CostEstimate(
                flops=4 * update.size, bytes_accessed=20 * 2**20, transcendentals=0
            ),
            compiler_params=params(),
            name="advance_states",
        )(me, state_place, store_place, update, decay_row, *state_gots)
        return gots, prior, final_sends

    page_gots, prior, final_sends = lax.switch(
        choice,
        [functools.partial(advance, at) for at in range(len(counts))],
        tuple(page_sends),
        state_gots,
        update,
        decay_row,
    )
    final_gots = [final_sends[0]] + [
        send_to(distance, final_sends[distance]) for distance in distances
    ]
    mixer_out = pl.pallas_call(
        functools.partial(output_kernel, per_group),
        grid=(requests, groups),
        in_specs=[
            x_block,
            map_block,
            column_block,
            pl.BlockSpec((None, None, group_width, state), lambda r, g: (r, g, 0, 0)),
        ],
        out_specs=x_block,
        out_shape=jax.ShapeDtypeStruct((requests * length, width), jnp.bfloat16),
        cost_estimate=pl.CostEstimate(
            flops=2 * requests * length * width * state,
            bytes_accessed=18 * 2**20,
            transcendentals=0,
        ),
        compiler_params=params(),
        name="add_carried",
    )(partial, output_map, growth_col, prior)
    passed = pass_on(counts, limits, page_place, prefix_tokens, pages_by_head, page_gots)
    stored = None
    for distance, got in enumerate(final_gots):
        if distance == peers - 1:
            passed, stored = lax.optimization_barrier((passed, stored))
        stored = scatter_from(
            ends(peers - distance), store_place, got, stored, state_pool.shape
        )
    rows = per_kv * length
    head_block = pl.BlockSpec(
        (None, None, per_kv, length, attend_dim), lambda r, e, *_: (r, e, 0, 0, 0)
    )
    sums_block = pl.BlockSpec((None, None, attend_dim, rows), lambda r, e, *_: (r, e, 0, 0))
    stats_block = pl.BlockSpec((None, None, 2, rows), lambda r, e, *_: (r, e, 0, 0))
    lists = [
        pltpu.SMEM((requests * prefix_pages,), jnp.int32),
        pltpu.SMEM((requests * prefix_pages,), jnp.int32),
        pltpu.SMEM((requests,), jnp.int32),
        pltpu.SMEM((requests,), jnp.int32),
        pltpu.SMEM((2, peers), jnp.int32),
    ]
    sums, stats = pl.pallas_call(
        functools.partial(attend_kernel, attend_dim**-0.5, counts),
        grid_spec=pltpu.PrefetchScalarGridSpec(
            num_scalar_prefetch=3,
            grid=(requests, kv_heads),
            in_specs=[any_spec()] * (len(page_gots) + 1)
            + [
                head_block,
                pl.BlockSpec((None, length, 2 * attend_dim), lambda r, e, *_: (e, r, 0)),
            ],
            out_specs=[sums_block, stats_block],
            scratch_shapes=[
                pltpu.VMEM((prefix_pages * page, 2 * attend_dim), jnp.bfloat16),
                *lists,
                pltpu.SemaphoreType.DMA((prefix_pages,)),
            ],
        ),
        out_shape=[
            jax.ShapeDtypeStruct((requests, kv_heads, attend_dim, rows), jnp.float32),
            jax.ShapeDtypeStruct((requests, kv_heads, 2, rows), jnp.float32),
        ],
        cost_estimate=pl.CostEstimate(
            flops=4 * queries.size * (prefix_pages * page + length),
            bytes_accessed=16 * 2**20,
            transcendentals=queries.shape[0] * queries.shape[1] * (prefix_pages * page),
        ),
        compiler_params=params(),
        name="attend",
    )(
        limits,
        page_place,
        prefix_tokens,
        pages_by_head,
        *page_gots,
        grouped_queries,
        fresh,
    )
    attended = pl.pallas_call(
        functools.partial(attend_passed_kernel, attend_dim**-0.5, counts, page_slots),
        grid_spec=pltpu.PrefetchScalarGridSpec(
            num_scalar_prefetch=3,
            grid=(requests, kv_heads),
            in_specs=[any_spec(), head_block, sums_block, stats_block],
            out_specs=head_block,
            scratch_shapes=[
                pltpu.VMEM((-(-PASSED * page // length) * length, 2 * attend_dim), jnp.bfloat16),
                pltpu.VMEM((attend_dim, rows), jnp.float32),
                pltpu.VMEM((2, rows), jnp.float32),
                *lists,
                pltpu.SemaphoreType.DMA((PASSED,)),
            ],
        ),
        out_shape=jax.ShapeDtypeStruct(grouped_queries.shape, jnp.bfloat16),
        cost_estimate=pl.CostEstimate(
            flops=queries.size * PASSED * page,
            bytes_accessed=8 * 2**20,
            transcendentals=queries.shape[0] * queries.shape[1] * PASSED * page // 4,
        ),
        compiler_params=params(),
        name="attend_passed",
    )(limits, page_place, prefix_tokens, passed, grouped_queries, sums, stats)
    attention_out = attended.transpose(0, 3, 1, 2, 4).reshape(queries.shape)
    return mixer_out, attention_out, stored


def solution(mesh):
    placed = (
        P(("parts", "req"), "tp"),
        P(("parts", "req"), "tp", None),
        P(("parts", "req"), "tp"),
        P(("parts", "req"), None, "tp"),
        P(("parts", "req"), None, "tp", None),
        P(None, "tp"),
        P(None, "tp", None),
        P("tp"),
        P("tp"),
        P(("parts", "req"), "tp", None, None),
        P(("parts", "req"), "tp", None),
        P(("parts", "req"), "tp", None),
        P(("parts", "req"), None, "tp", None),
        P("parts"),
        P("parts", None),
        P("parts", None),
        P("parts", None),
    )
    return jax.shard_map(
        body,
        mesh=mesh,
        in_specs=placed,
        out_specs=(
            P(("parts", "req"), "tp"),
            P(("parts", "req"), "tp", None),
            P(("parts", "req"), "tp", None, None),
        ),
        check_vma=False,
    )
```

profile of v0, /device:TPU:14, one launch (start us, length us, event | category | flops | bytes accessed | tf_op | source)
XLA Modules:
  0.0 247.9 jit_solution(9340243731995186368)
XLA Ops:
  0.7 3.2 %gather_states.3 = bf16[16,32,4,256]{3,2,1,0:T(4,128)(2,1)} custom-call(s32[2]{0:T(128)S(1)} %pad_add_fusion.1.ends_ref, s32[16,16]{1,0:T(8,128)} %place_ref.14, bf16[64,32,4,256]{3,2,1,0:T(4,128)(2,1)} %pool_ref.5), custom_call_target="tpu_custom_call" | custom-call | bytes 2097152 | tf_op jit(solution)/shard_map/gather_states/pallas_call | solution.py:64
  4.0 1.7 collective-permute-start
  5.7 3.0 %gather_states.4 = bf16[16,32,4,256]{3,2,1,0:T(4,128)(2,1)} custom-call(s32[2]{0:T(128)S(1)} %pad_add_fusion.2.ends_ref, s32[16,16]{1,0:T(8,128)S(1)} %copy-done.18, bf16[64,32,4,256]{3,2,1,0:T(4,128)(2,1)} %pool_ref.5), custom_call_target="tpu_custom_call" | custom-call | bytes 2097152 | tf_op jit(solution)/shard_map/gather_states/pallas_call | solution.py:64
  8.7 1.3 collective-permute-start.1
  10.1 3.0 %gather_states.5 = bf16[16,32,4,256]{3,2,1,0:T(4,128)(2,1)} custom-call(s32[2]{0:T(128)S(1)} %pad_add_fusion.3.ends_ref, s32[16,16]{1,0:T(8,128)S(1)} %copy-done.18, bf16[64,32,4,256]{3,2,1,0:T(4,128)(2,1)} %pool_ref.5), custom_call_target="tpu_custom_call" | custom-call | bytes 2097152 | tf_op jit(solution)/shard_map/gather_states/pallas_call | solution.py:64
  13.1 1.8 collective-permute-start.2
  15.3 2.3 reduce-window.6
  19.2 0.6 fusion.9
  19.9 1.3 fusion.10
  21.2 1.3 fusion.11
  22.4 0.7 copy_exponential_fusion
  23.1 1.4 pad_add_fusion.limits_ref
  24.5 1.4 copy.101
  26.0 1.4 copy.107
  27.3 5.3 %copy.129 = bf16[64,64,2,256]{3,1,2,0:T(8,128)(2,1)} copy(bf16[64,64,2,256]{3,2,1,0:T(2,128)(2,1)} %param.37) | data formatting | bytes 8388608 | tf_op args[12]
  32.6 0.7 copy.95
  33.3 0.3 copy.131
  33.7 1.3 copy.106
  35.1 1.2 copy.109
  37.0 2.2 copy-done
  39.2 8.3 %send_used_pages.1 = (bf16[24,2,64,256]{3,2,1,0:T(8,128)(2,1)}, bf16[28,2,64,256]{3,2,1,0:T(8,128)(2,1)}, bf16[32,2,64,256]{3,2,1,0:T(8,128)(2,1)}, bf16[36,2,64...) custom-call(s32[3]{0:T(128)S(1)} %pad_add_fusion.limits_ref, ...), custom_call_target="tpu_custom_call" | custom-call | bytes 8388608 | tf_op jit(solution)/shard_map/send_used_pages/pallas_call | solution.py:237
  47.6 1.0 pad_convert_fusion.x_cache_ref
  48.8 37.8 %mix_new_tokens.1 = (f32[1024,2048]{1,0:T(8,128)}, f32[4,2,1024,256]{3,2,1,0:T(8,128)}, bf16[2,1024,256]{2,1,0:T(8,128)(2,1)S(1)}) custom-call(bf16[1024,2048]{1,0:T(8,128)(2,1)} %x_ref.1, f32[4,8,2048]{2,1,0:T(8,128)S(1)} %pad_convert_fusion.x_cache_ref, f32[4,2048]{1,0:T(4,128)S(1)} %convert_element_type.31.x_weight_ref, ...), custom_call_target="tpu_custom_call" | custom-call | flops 1610612736 | bytes 33554432 | tf_op jit(solution)/shard_map/mix_new_tokens/pallas_call | solution.py:840
  86.7 1.0 copy-done.2
  87.7 8.1 %collective-permute-done.1 = bf16[16,32,4,256]{3,2,1,0:T(4,128)(2,1)} collective-permute-done((bf16[16,32,4,256]{3,2,1,0:T(4,128)(2,1)}, bf16[16,32,4,256]{3,2,1,0:T(4,128)(2,1)}, u32[]{:S(2)}, u32[]{:S(2)}) %collective-permute-start.1) | collective-permute-done | bytes 1048608 | tf_op jit(solution)/shard_map/ppermute | solution.py:786
  95.8 1.8 collective-permute-done.2
  97.6 44.9 %conditional.1 = (bf16[24,2,64,256]{3,2,1,0:T(8,128)(2,1)}, bf16[28,2,64,256]{3,2,1,0:T(8,128)(2,1)}, bf16[32,2,64,256]{3,2,1,0:T(8,128)(2,1)}, bf16[36,2,64,256...) conditional(s32[]{:T(128)} %clamp.3, ...), branch_computations={%region_9.10_spmd, %region_10.11_spmd, %region_11.12_spmd, %region... | conditional | flops 8388608 | bytes 35651740 | solution.py:937
  97.6 4.3 %all-to-all-start.1 = ((bf16[28,2,64,256]{3,2,1,0:T(8,128)(2,1)}), bf16[28,2,64,256]{3,2,1,0:T(8,128)(2,1)S(1)}, u32[]{:S(2)}, u32[]{:S(2)}) async-start(bf16[28,2,64,256]{3,2,1,0:T(8,128)(2,1)} %get-tuple-element.162), calls=%async_computation.1 | async-start | bytes 3670016 | tf_op jit(solution)/shard_map/cond/branch_1_fun/all_to_all | solution.py:780
  101.9 24.8 %advance_states.8 = (bf16[4,2,1024,256]{3,2,1,0:T(8,128)(2,1)}, bf16[16,32,4,256]{3,2,1,0:T(4,128)(2,1)}, bf16[16,32,4,256]{3,2,1,0:T(4,128)(2,1)}, bf16[16,32,4...) custom-call(s32[1]{0:T(128)} %get-tuple-element.168.me_ref, s32[16,16]{1,0:T(8,128)S(1)} %get-tuple-element.169.state_place_ref, ...), custom_call_target="tpu_custom_call" | custom-call | flops 8388608 | bytes 20971520 | tf_op jit(solution)/shard_map/cond/branch_1_fun/advance_states/pallas_call | solution.py:905
  126.7 14.5 %all-to-all-done.1 = bf16[28,2,64,256]{3,2,1,0:T(8,128)(2,1)S(1)} async-done(((bf16[28,2,64,256]{3,2,1,0:T(8,128)(2,1)}), bf16[28,2,64,256]{3,2,1,0:T(8,128)(2,1)S(1)}, u32[]{:S(2)}, u32[]{:S(2)}) %all-to-all-start.1) | async-done | bytes 1835040 | tf_op jit(solution)/shard_map/cond/branch_1_fun/all_to_all | solution.py:780
  141.2 1.3 copy-done.11
  142.4 0.6 collective-permute-start.5
  143.1 4.2 %collective-permute-start.4 = (bf16[16,32,4,256]{3,2,1,0:T(4,128)(2,1)}, bf16[16,32,4,256]{3,2,1,0:T(4,128)(2,1)S(1)}, u32[]{:S(2)}, u32[]{:S(2)}) collective-permute-start(bf16[16,32,4,256]{3,2,1,0:T(4,128)(2,1)} %get-tuple-element.366), channel_id=1, source_target_pairs={{0,8},{4,12},{8,0},{12,4},{1,9},{5,13},{9,1},{13,5},{2,10},{6,14},... | collective-permute-start | bytes 3145736 | tf_op jit(solution)/shard_map/ppermute | solution.py:786
  147.2 0.5 collective-permute-start.6
  147.7 2.3 copy.130
  150.0 1.4 copy.132
  151.5 3.5 %pass_pages_on.1 = bf16[8,2,64,256]{3,2,1,0:T(8,128)(2,1)} custom-call(s32[3]{0:T(128)S(1)} %pad_add_fusion.limits_ref, s32[16,16]{1,0:T(8,128)S(1)} %copy-done.5, s32[16]{0:T(128)S(1)} %copy-done.6, bf16[64,2,64,256]{3,2,1,0:T(8,128)(2,1)S(1)} %bitcast.64, bf16[24,2,64,256]{3,2,1,0:T(8,128)(2,1)S(1)} %copy-done.8, ...), custom_call_target="tpu_custom_call" | custom-call | bytes 1048576 | tf_op jit(solution)/shard_map/pass_pages_on/pallas_call | solution.py:326
  155.1 1.7 collective-permute-start.3
  156.8 10.8 %add_carried.1 = bf16[1024,2048]{1,0:T(8,128)(2,1)} custom-call(f32[1024,2048]{1,0:T(8,128)} %get-tuple-element.342.partial_ref, bf16[2,1024,256]{2,1,0:T(8,128)(2,1)S(1)} %copy-done.3, f32[4,2,256,16]{3,2,1,0:T(8,128)S(1)} %bitcast.68, bf16[4,2,1024,256]{3,2,1,0:T(8,128)(2,1)} %get-tuple-element.358.prior_ref), custom_call_target="tpu_custom_call" | custom-call | flops 1073741824 | bytes 18874368 | tf_op jit(solution)/shard_map/add_carried/pallas_call | solution.py:948
  167.6 1.7 scatter_states.4.rest_0_
  169.4 0.7 copy-done.12
  170.1 27.9 %attend.1 = (f32[4,2,128,1024]{3,2,1,0:T(8,128)}, f32[4,2,2,1024]{3,2,1,0:T(2,128)S(1)}) custom-call(s32[3]{0:T(128)S(1)} %pad_add_fusion.limits_ref, s32[16,16]{1,0:T(8,128)S(1)} %copy-done.5, s32[16]{0:T(128)S(1)} %copy-done.6, bf16[64,2,64,256]{3,2,1,0:T(8,128)(2,1)} %bitcast.62, bf16[24,2,64,256]{3,2,1,0:T(8,128)(2,1)S(1)} %copy-done.8, ...), custom_call_target="tpu_custom_call" | custom-call | flops 5368709120 | bytes 16777216 | tf_op jit(solution)/shard_map/attend/pallas_call | solution.py:988
  198.1 1.7 scatter_states.5.rest_0_
  199.8 32.6 %collective-permute-done.4.got_ref = bf16[16,32,4,256]{3,2,1,0:T(4,128)(2,1)S(1)} collective-permute-done((bf16[16,32,4,256]{3,2,1,0:T(4,128)(2,1)}, bf16[16,32,4,256]{3,2,1,0:T(4,128)(2,1)S(1)}, u32[]{:S(2)}, u32[]{:S(2)}) %collective-permute-start.4) | collective-permute-done | bytes 1048608 | tf_op jit(solution)/shard_map/ppermute | solution.py:786
  232.4 1.7 scatter_states.6.rest_0_
  234.2 9.0 %attend_passed.1 = bf16[4,2,4,256,128]{4,3,2,1,0:T(8,128)(2,1)S(1)} custom-call(s32[3]{0:T(128)S(1)} %pad_add_fusion.limits_ref, s32[16,16]{1,0:T(8,128)S(1)} %copy-done.5, s32[16]{0:T(128)S(1)} %copy-done.6, bf16[8,2,64,256]{3,2,1,0:T(8,128)(2,1)S(1)} %collective-permute-done.3.passed_ref, bf16[4,2,4,256,128]{4,3,2,1,0:T(8,128)(2,1)S(1)} %bitcast.66, ...), custom_call_target="tpu_custom_call" | custom-call | flops 536870912 | bytes 8388608 | tf_op jit(solution)/shard_map/attend_passed/pallas_call | solution.py:1025
  243.3 2.7 %copy.114 = bf16[1024,8,128]{2,1,0:T(8,128)(2,1)} copy(bf16[1024,8,128]{2,0,1:T(8,128)(2,1)S(1)} %bitcast.81) | data formatting | bytes 4194304
  246.0 1.7 scatter_states.7
  (98 shorter events, 2.9 us)
Async XLA Ops:
  0.7 5.0 %copy-start.18 = (s32[16,16]{1,0:T(8,128)S(1)}, s32[16,16]{1,0:T(8,128)}, u32[]{:S(2)}) copy-start(s32[16,16]{1,0:T(8,128)} %place_ref.14) | copy-start | bytes 3076
  4.0 83.7 %collective-permute-start = (bf16[16,32,4,256]{3,2,1,0:T(4,128)(2,1)}, bf16[16,32,4,256]{3,2,1,0:T(4,128)(2,1)}, u32[]{:S(2)}, u32[]{:S(2)}) collective-permute-start(bf16[16,32,4,256]{3,2,1,0:T(4,128)(2,1)} %gather_states.3), channel_id=1, source_target_pairs={{0,4},{4,8},{8,12},{12,0},{1,5},{5,9},{9,13},{13,1},{2,6},{6,10},{... | collective-permute-start | bytes 3145736 | tf_op jit(solution)/shard_map/ppermute | solution.py:786
  8.7 87.0 %collective-permute-start.1 = (bf16[16,32,4,256]{3,2,1,0:T(4,128)(2,1)}, bf16[16,32,4,256]{3,2,1,0:T(4,128)(2,1)}, u32[]{:S(2)}, u32[]{:S(2)}) collective-permute-start(bf16[16,32,4,256]{3,2,1,0:T(4,128)(2,1)} %gather_states.4), channel_id=1, source_target_pairs={{0,8},{4,12},{8,0},{12,4},{1,9},{5,13},{9,1},{13,5},{2,10},{6,14},... | collective-permute-start | bytes 3145736 | tf_op jit(solution)/shard_map/ppermute | solution.py:786
  10.1 4.9 %copy-start.19 = (bf16[1024,32]{0,1:T(8,128)(2,1)S(1)}, bf16[1024,32]{0,1:T(8,128)(2,1)}, u32[]{:S(2)}) copy-start(bf16[1024,32]{0,1:T(8,128)(2,1)} %param.27) | copy-start | bytes 196612
  10.1 5.1 %copy-start.27 = (f32[32]{0:T(128)S(1)}, f32[32]{0:T(128)}, u32[]{:S(2)}) copy-start(f32[32]{0:T(128)} %param.32) | copy-start | bytes 388
  10.1 7.9 %copy-start.5 = (s32[16,16]{1,0:T(8,128)S(1)}, s32[16,16]{1,0:T(8,128)}, u32[]{:S(2)}) copy-start(s32[16,16]{1,0:T(8,128)} %place_ref.20) | copy-start | bytes 3076
  10.1 8.1 %copy-start.6 = (s32[16]{0:T(128)S(1)}, s32[16]{0:T(128)}, u32[]{:S(2)}) copy-start(s32[16]{0:T(128)} %prefix_ref.7) | copy-start | bytes 196
  10.1 9.0 %copy-start.25 = (s32[7]{0:T(128)S(1)}, s32[7]{0:T(128)}, u32[]{:S(2)}) copy-start(s32[7]{0:T(128)} %constant.123) | copy-start | bytes 88
  10.1 9.8 %copy-start.26 = (s32[7]{0:T(128)S(1)}, s32[7]{0:T(128)}, u32[]{:S(2)}) copy-start(s32[7]{0:T(128)} %constant.122) | copy-start | bytes 88
  10.1 11.0 %copy-start.28 = (s32[7]{0:T(128)S(1)}, s32[7]{0:T(128)}, u32[]{:S(2)}) copy-start(s32[7]{0:T(128)} %constant.111.clone) | copy-start | bytes 88
  13.1 84.5 %collective-permute-start.2 = (bf16[16,32,4,256]{3,2,1,0:T(4,128)(2,1)}, bf16[16,32,4,256]{3,2,1,0:T(4,128)(2,1)}, u32[]{:S(2)}, u32[]{:S(2)}) collective-permute-start(bf16[16,32,4,256]{3,2,1,0:T(4,128)(2,1)} %gather_states.5), channel_id=1, source_target_pairs={{0,12},{4,0},{8,4},{12,8},{1,13},{5,1},{9,5},{13,9},{2,14},{6,2},{... | collective-permute-start | bytes 3145736 | tf_op jit(solution)/shard_map/ppermute | solution.py:786
  27.3 5.3 %copy-start.20 = (bf16[4,3,2048]{2,0,1:T(4,128)(2,1)S(1)}, bf16[4,3,2048]{2,0,1:T(4,128)(2,1)}, u32[]{:S(2)}) copy-start(bf16[4,3,2048]{2,0,1:T(4,128)(2,1)} %param.28) | copy-start | bytes 147460
  27.3 5.9 %copy-start.22 = (bf16[4,2048]{1,0:T(4,128)(2,1)S(1)}, bf16[4,2048]{1,0:T(4,128)(2,1)}, u32[]{:S(2)}) copy-start(bf16[4,2048]{1,0:T(4,128)(2,1)} %param.30) | copy-start | bytes 49156
  27.3 6.0 %copy-start.15 = (bf16[1024,2,512]{2,1,0:T(2,128)(2,1)S(1)}, bf16[1024,2,512]{2,1,0:T(2,128)(2,1)}, u32[]{:S(2)}) copy-start(bf16[1024,2,512]{2,1,0:T(2,128)(2,1)} %param.26) | copy-start | bytes 6291460
  32.6 1.1 copy-start.21
  33.3 1.7 copy-start.24
  35.1 12.5 %copy-start.23 = (bf16[4,2,512]{2,1,0:T(2,128)(2,1)S(1)}, bf16[4,2,512]{2,1,0:T(2,128)(2,1)}, u32[]{:S(2)}) copy-start(bf16[4,2,512]{2,1,0:T(2,128)(2,1)} %param.31) | copy-start | bytes 24580
  37.0 2.2 copy-start
  39.2 9.4 %copy-start.13 = (f32[2,16,4,256]{1,3,0,2:T(8,128)S(1)}, f32[2,16,4,256]{1,3,0,2:T(8,128)}, u32[]{:S(2)}) copy-start(f32[2,16,4,256]{1,3,0,2:T(8,128)} %copy.107) | copy-start | bytes 393220
  39.2 9.4 %copy-start.14 = (f32[2,16,4,256]{1,3,0,2:T(8,128)S(1)}, f32[2,16,4,256]{1,3,0,2:T(8,128)}, u32[]{:S(2)}) copy-start(f32[2,16,4,256]{1,3,0,2:T(8,128)} %copy.106) | copy-start | bytes 393220
  47.6 1.3 copy-start.4
  48.8 48.7 %copy-start.17 = (s32[16,16]{1,0:T(8,128)S(1)}, s32[16,16]{1,0:T(8,128)}, u32[]{:S(2)}) copy-start(s32[16,16]{1,0:T(8,128)} %place_ref.21) | copy-start | bytes 3076
  86.7 1.0 copy-start.2
  97.6 43.6 %all-to-all-start.1 = ((bf16[28,2,64,256]{3,2,1,0:T(8,128)(2,1)}), bf16[28,2,64,256]{3,2,1,0:T(8,128)(2,1)S(1)}, u32[]{:S(2)}, u32[]{:S(2)}) async-start(bf16[28,2,64,256]{3,2,1,0:T(8,128)(2,1)} %get-tuple-element.162), calls=%async_computation.1 | async-start | bytes 3670016 | tf_op jit(solution)/shard_map/cond/branch_1_fun/all_to_all | solution.py:780
  141.2 1.3 copy-start.11
  142.4 55.6 %collective-permute-start.5 = (bf16[16,32,4,256]{3,2,1,0:T(4,128)(2,1)}, bf16[16,32,4,256]{3,2,1,0:T(4,128)(2,1)S(1)}, u32[]{:S(2)}, u32[]{:S(2)}) collective-permute-start(bf16[16,32,4,256]{3,2,1,0:T(4,128)(2,1)} %get-tuple-element.367), channel_id=1, source_target_pairs={{0,4},{4,8},{8,12},{12,0},{1,5},{5,9},{9,13},{13,1},{2,6},{6,10},{... | collective-permute-start | bytes 3145736 | tf_op jit(solution)/shard_map/ppermute | solution.py:786
  143.1 89.4 %collective-permute-start.4 = (bf16[16,32,4,256]{3,2,1,0:T(4,128)(2,1)}, bf16[16,32,4,256]{3,2,1,0:T(4,128)(2,1)S(1)}, u32[]{:S(2)}, u32[]{:S(2)}) collective-permute-start(bf16[16,32,4,256]{3,2,1,0:T(4,128)(2,1)} %get-tuple-element.366), channel_id=1, source_target_pairs={{0,8},{4,12},{8,0},{12,4},{1,9},{5,13},{9,1},{13,5},{2,10},{6,14},... | collective-permute-start | bytes 3145736 | tf_op jit(solution)/shard_map/ppermute | solution.py:786
  147.2 98.8 %collective-permute-start.6 = (bf16[16,32,4,256]{3,2,1,0:T(4,128)(2,1)}, bf16[16,32,4,256]{3,2,1,0:T(4,128)(2,1)S(1)}, u32[]{:S(2)}, u32[]{:S(2)}) collective-permute-start(bf16[16,32,4,256]{3,2,1,0:T(4,128)(2,1)} %get-tuple-element.372), channel_id=1, source_target_pairs={{0,12},{4,0},{8,4},{12,8},{1,13},{5,1},{9,5},{13,9},{2,14},{6,2},{... | collective-permute-start | bytes 3145736 | tf_op jit(solution)/shard_map/ppermute | solution.py:786
  147.7 3.8 %copy-start.1 = (bf16[64,64,2,256]{3,1,2,0:T(8,128)(2,1)S(1)}, bf16[64,64,2,256]{3,1,2,0:T(8,128)(2,1)}, u32[]{:S(2)}) copy-start(bf16[64,64,2,256]{3,1,2,0:T(8,128)(2,1)} %copy.129) | copy-start | bytes 12582916
  147.7 3.8 %copy-start.8 = (bf16[24,2,64,256]{3,2,1,0:T(8,128)(2,1)S(1)}, bf16[24,2,64,256]{3,2,1,0:T(8,128)(2,1)}, u32[]{:S(2)}) copy-start(bf16[24,2,64,256]{3,2,1,0:T(8,128)(2,1)} %get-tuple-element.359.rest_0_) | copy-start | bytes 4718596
  151.5 5.3 %copy-start.3 = (bf16[2,1024,256]{2,1,0:T(8,128)(2,1)S(1)}, bf16[2,1024,256]{2,1,0:T(8,128)(2,1)}, u32[]{:S(2)}) copy-start(bf16[2,1024,256]{2,1,0:T(8,128)(2,1)} %copy-done.2) | copy-start | bytes 3145732
  155.1 79.1 %collective-permute-start.3 = (bf16[8,2,64,256]{3,2,1,0:T(8,128)(2,1)}, bf16[8,2,64,256]{3,2,1,0:T(8,128)(2,1)S(1)}, u32[]{:S(2)}, u32[]{:S(2)}) collective-permute-start(bf16[8,2,64,256]{3,2,1,0:T(8,128)(2,1)} %pass_pages_on.1), channel_id=1, source_target_pairs={{0,4},{4,0},{8,12},{12,8},{1,5},{5,1},{9,13},{13,9},{2,6},{6,2},{1... | collective-permute-start | bytes 1572872 | tf_op jit(solution)/shard_map/ppermute | solution.py:345
  156.8 10.8 %copy-start.16 = (bf16[16,32,4,256]{3,2,1,0:T(4,128)(2,1)S(1)}, bf16[16,32,4,256]{3,2,1,0:T(4,128)(2,1)}, u32[]{:S(2)}) copy-start(bf16[16,32,4,256]{3,2,1,0:T(4,128)(2,1)} %get-tuple-element.368.got_ref) | copy-start | bytes 3145732
  167.6 1.8 copy-start.10
  167.6 2.5 %copy-start.12 = (bf16[28,2,64,256]{3,2,1,0:T(8,128)(2,1)S(1)}, bf16[28,2,64,256]{3,2,1,0:T(8,128)(2,1)}, u32[]{:S(2)}) copy-start(bf16[28,2,64,256]{3,2,1,0:T(8,128)(2,1)} %get-tuple-element.360.rest_1_) | copy-start | bytes 5505028
where the time goes:
time: 252 us; the launch traced here: 248 us
  Pallas kernels  138 us (55%)
  waiting for transfers between devices  57.1 us (23%)
  local copies, waits for them, and re-layouts  24.8 us (10%)
  starting transfers between devices  16.2 us (6%)
  other arithmetic  9.65 us (4%)
    ppermute x6, waiting for transfers between devices, send_to(): lax.ppermute(pages, 'req', [(peer, (peer + distance) % peers) for peer in...  42.6 us
    pallas_call x1, Pallas kernels, body(): pl.pallas_call(functools.partial(inner_kernel, per_group), grid=(requests...  37.8 us
    pallas_call x1, Pallas kernels, body(): pl.pallas_call(functools.partial(attend_kernel, attend_dim ** (-0.5), cou...  27.9 us
    pallas_call x1, Pallas kernels, advance(): pl.pallas_call(state_kernel, grid_spec=pltpu.PrefetchScalarGridSpec(num_s...  24.8 us
    all_to_all x1, waiting for transfers between devices, exchange(): return lax.all_to_all(pages, 'req', split_axis=0, concat_axis=0, tiled=True)  14.5 us
    unnamed x58, local copies, waits for them, and re-layouts  14.5 us
    pallas_call x1, Pallas kernels, body(): pl.pallas_call(functools.partial(output_kernel, per_group), grid=(request...  10.8 us
    ppermute x6, starting transfers between devices, send_to(): lax.ppermute(pages, 'req', [(peer, (peer + distance) % peers) for peer in...  10.1 us
  transfers between devices with their start and end apart: 8, of which 4 were waited for; matrix products, arithmetic and copies ran while one was open for 12% of the time, Pallas kernels for 54%

commit v1 on v0

--- a/solution.py
+++ b/solution.py
@@ -967,7 +967,7 @@
     passed = pass_on(counts, limits, page_place, prefix_tokens, pages_by_head, page_gots)
     stored = None
     for distance, got in enumerate(final_gots):
-        if distance == peers - 1:
+        if distance == min(2, peers - 1):
             passed, stored = lax.optimization_barrier((passed, stored))
         stored = scatter_from(
             ends(peers - distance), store_place, got, stored, state_pool.shape

time: 252 us -> 249 us (0.988)
  the two profiles are of different devices: /device:TPU:14 before, /device:TPU:4 now
where the time goes in v1:
time: 249 us; the launch traced here: 245 us
  Pallas kernels  133 us (53%)
  waiting for transfers between devices  52.8 us (21%)
  local copies, waits for them, and re-layouts  25 us (10%)
  starting transfers between devices  23 us (9%)
  other arithmetic  9.65 us (4%)
    pallas_call x1, Pallas kernels, body(): pl.pallas_call(functools.partial(inner_kernel, per_group), grid=(requests...  37.8 us
    ppermute x1, waiting for transfers between devices, pass_on(): return lax.ppermute(collected, 'req', swaps)  30.1 us
    pallas_call x1, Pallas kernels, advance(): pl.pallas_call(state_kernel, grid_spec=pltpu.PrefetchScalarGridSpec(num_s...  24.7 us
    pallas_call x1, Pallas kernels, body(): pl.pallas_call(functools.partial(attend_kernel, attend_dim ** (-0.5), cou...  24 us
    all_to_all x1, waiting for transfers between devices, exchange(): return lax.all_to_all(pages, 'req', split_axis=0, concat_axis=0, tiled=True)  22.6 us
    unnamed x58, local copies, waits for them, and re-layouts  14.5 us
    all_to_all x1, starting transfers between devices, exchange(): return lax.all_to_all(pages, 'req', split_axis=0, concat_axis=0, tiled=True)  12.5 us
    pallas_call x1, Pallas kernels, body(): pl.pallas_call(functools.partial(output_kernel, per_group), grid=(request...  10.8 us
  transfers between devices with their start and end apart: 8, of which 2 were waited for; matrix products, arithmetic and copies ran while one was open for 12% of the time, Pallas kernels for 52%

profile of v1, /device:TPU:4, one launch (start us, length us, event | category | flops | bytes accessed | tf_op | source)
XLA Modules:
  0.0 245.4 jit_solution(13082302780123691622)
XLA Ops:
  0.7 3.2 %gather_states.3 = bf16[16,32,4,256]{3,2,1,0:T(4,128)(2,1)} custom-call(s32[2]{0:T(128)S(1)} %pad_add_fusion.1.ends_ref, s32[16,16]{1,0:T(8,128)} %place_ref.14, bf16[64,32,4,256]{3,2,1,0:T(4,128)(2,1)} %pool_ref.5), custom_call_target="tpu_custom_call" | custom-call | bytes 2097152 | tf_op jit(solution)/shard_map/gather_states/pallas_call | solution.py:64
  4.0 1.7 collective-permute-start
  5.7 3.0 %gather_states.4 = bf16[16,32,4,256]{3,2,1,0:T(4,128)(2,1)} custom-call(s32[2]{0:T(128)S(1)} %pad_add_fusion.2.ends_ref, s32[16,16]{1,0:T(8,128)S(1)} %copy-done.18, bf16[64,32,4,256]{3,2,1,0:T(4,128)(2,1)} %pool_ref.5), custom_call_target="tpu_custom_call" | custom-call | bytes 2097152 | tf_op jit(solution)/shard_map/gather_states/pallas_call | solution.py:64
  8.7 2.6 %collective-permute-start.1 = (bf16[16,32,4,256]{3,2,1,0:T(4,128)(2,1)}, bf16[16,32,4,256]{3,2,1,0:T(4,128)(2,1)}, u32[]{:S(2)}, u32[]{:S(2)}) collective-permute-start(bf16[16,32,4,256]{3,2,1,0:T(4,128)(2,1)} %gather_states.4), channel_id=1, source_target_pairs={{0,8},{4,12},{8,0},{12,4},{1,9},{5,13},{9,1},{13,5},{2,10},{6,14},... | collective-permute-start | bytes 3145736 | tf_op jit(solution)/shard_map/ppermute | solution.py:786
  11.5 3.0 %gather_states.5 = bf16[16,32,4,256]{3,2,1,0:T(4,128)(2,1)} custom-call(s32[2]{0:T(128)S(1)} %pad_add_fusion.3.ends_ref, s32[16,16]{1,0:T(8,128)S(1)} %copy-done.18, bf16[64,32,4,256]{3,2,1,0:T(4,128)(2,1)} %pool_ref.5), custom_call_target="tpu_custom_call" | custom-call | bytes 2097152 | tf_op jit(solution)/shard_map/gather_states/pallas_call | solution.py:64
  14.5 1.4 collective-permute-start.2
  16.2 2.3 reduce-window.6
  18.5 0.2 slice_reduce_fusion
  19.6 0.2 slice_reduce_fusion.1
  20.2 0.6 fusion.9
  20.8 1.3 fusion.10
  22.1 1.3 fusion.11
  23.3 0.7 copy_exponential_fusion
  24.0 1.4 pad_add_fusion.limits_ref
  25.4 1.4 copy.101
  26.9 1.4 copy.107
  28.2 5.3 %copy.129 = bf16[64,64,2,256]{3,1,2,0:T(8,128)(2,1)} copy(bf16[64,64,2,256]{3,2,1,0:T(2,128)(2,1)} %param.37) | data formatting | bytes 8388608 | tf_op args[12]
  33.5 0.7 copy.95
  34.2 0.3 copy.131
  34.6 1.3 copy.106
  36.0 1.2 copy.109
  37.9 2.2 copy-done
  40.1 8.7 %send_used_pages.1 = (bf16[24,2,64,256]{3,2,1,0:T(8,128)(2,1)}, bf16[28,2,64,256]{3,2,1,0:T(8,128)(2,1)}, bf16[32,2,64,256]{3,2,1,0:T(8,128)(2,1)}, bf16[36,2,64...) custom-call(s32[3]{0:T(128)S(1)} %pad_add_fusion.limits_ref, ...), custom_call_target="tpu_custom_call" | custom-call | bytes 8388608 | tf_op jit(solution)/shard_map/send_used_pages/pallas_call | solution.py:237
  48.9 1.0 pad_convert_fusion.x_cache_ref
  50.1 37.8 %mix_new_tokens.1 = (f32[1024,2048]{1,0:T(8,128)}, f32[4,2,1024,256]{3,2,1,0:T(8,128)}, bf16[2,1024,256]{2,1,0:T(8,128)(2,1)S(1)}) custom-call(bf16[1024,2048]{1,0:T(8,128)(2,1)} %x_ref.1, f32[4,8,2048]{2,1,0:T(8,128)S(1)} %pad_convert_fusion.x_cache_ref, f32[4,2048]{1,0:T(4,128)S(1)} %convert_element_type.31.x_weight_ref, ...), custom_call_target="tpu_custom_call" | custom-call | flops 1610612736 | bytes 33554432 | tf_op jit(solution)/shard_map/mix_new_tokens/pallas_call | solution.py:840
  87.9 1.0 copy-done.2
  88.9 61.2 %conditional.1 = (bf16[24,2,64,256]{3,2,1,0:T(8,128)(2,1)}, bf16[28,2,64,256]{3,2,1,0:T(8,128)(2,1)}, bf16[32,2,64,256]{3,2,1,0:T(8,128)(2,1)}, bf16[36,2,64,256...) conditional(s32[]{:T(128)} %clamp.3, ...), branch_computations={%region_9.10_spmd, %region_10.11_spmd, %region_11.12_spmd, %region... | conditional | flops 8388608 | bytes 35651740 | solution.py:937
  88.9 12.5 %all-to-all-start.2 = ((bf16[32,2,64,256]{3,2,1,0:T(8,128)(2,1)}), bf16[32,2,64,256]{3,2,1,0:T(8,128)(2,1)S(1)}, u32[]{:S(2)}, u32[]{:S(2)}) async-start(bf16[32,2,64,256]{3,2,1,0:T(8,128)(2,1)} %get-tuple-element.184), calls=%async_computation.2 | async-start | bytes 4194304 | tf_op jit(solution)/shard_map/cond/branch_2_fun/all_to_all | solution.py:780
  101.4 24.7 %advance_states.9 = (bf16[4,2,1024,256]{3,2,1,0:T(8,128)(2,1)}, bf16[16,32,4,256]{3,2,1,0:T(4,128)(2,1)}, bf16[16,32,4,256]{3,2,1,0:T(4,128)(2,1)}, bf16[16,32,4...) custom-call(s32[1]{0:T(128)} %get-tuple-element.189.me_ref, s32[16,16]{1,0:T(8,128)S(1)} %get-tuple-element.190.state_place_ref, ...), custom_call_target="tpu_custom_call" | custom-call | flops 8388608 | bytes 20971520 | tf_op jit(solution)/shard_map/cond/branch_2_fun/advance_states/pallas_call | solution.py:905
  126.2 22.6 %all-to-all-done.2 = bf16[32,2,64,256]{3,2,1,0:T(8,128)(2,1)S(1)} async-done(((bf16[32,2,64,256]{3,2,1,0:T(8,128)(2,1)}), bf16[32,2,64,256]{3,2,1,0:T(8,128)(2,1)S(1)}, u32[]{:S(2)}, u32[]{:S(2)}) %all-to-all-start.2) | async-done | bytes 2097184 | tf_op jit(solution)/shard_map/cond/branch_2_fun/all_to_all | solution.py:780
  148.8 1.3 copy-done.9
  150.1 2.9 %collective-permute-start.6 = (bf16[16,32,4,256]{3,2,1,0:T(4,128)(2,1)}, bf16[16,32,4,256]{3,2,1,0:T(4,128)(2,1)S(1)}, u32[]{:S(2)}, u32[]{:S(2)}) collective-permute-start(bf16[16,32,4,256]{3,2,1,0:T(4,128)(2,1)} %get-tuple-element.372), channel_id=1, source_target_pairs={{0,8},{4,12},{8,0},{12,4},{1,9},{5,13},{9,1},{13,5},{2,10},{6,14},... | collective-permute-start | bytes 3145736 | tf_op jit(solution)/shard_map/ppermute | solution.py:786
  153.0 0.9 collective-permute-start.5
  153.9 2.3 copy.130
  156.2 1.4 copy.132
  157.8 3.5 %pass_pages_on.1 = bf16[8,2,64,256]{3,2,1,0:T(8,128)(2,1)} custom-call(s32[3]{0:T(128)S(1)} %pad_add_fusion.limits_ref, s32[16,16]{1,0:T(8,128)S(1)} %copy-done.5, s32[16]{0:T(128)S(1)} %copy-done.6, bf16[64,2,64,256]{3,2,1,0:T(8,128)(2,1)S(1)} %bitcast.64, bf16[24,2,64,256]{3,2,1,0:T(8,128)(2,1)S(1)} %copy-done.8, ...), custom_call_target="tpu_custom_call" | custom-call | bytes 1048576 | tf_op jit(solution)/shard_map/pass_pages_on/pallas_call | solution.py:326
  161.3 1.0 collective-permute-start.3
  162.3 10.8 %add_carried.1 = bf16[1024,2048]{1,0:T(8,128)(2,1)} custom-call(f32[1024,2048]{1,0:T(8,128)} %get-tuple-element.342.partial_ref, bf16[2,1024,256]{2,1,0:T(8,128)(2,1)S(1)} %copy-done.3, f32[4,2,256,16]{3,2,1,0:T(8,128)S(1)} %bitcast.68, bf16[4,2,1024,256]{3,2,1,0:T(8,128)(2,1)} %get-tuple-element.358.prior_ref), custom_call_target="tpu_custom_call" | custom-call | flops 1073741824 | bytes 18874368 | tf_op jit(solution)/shard_map/add_carried/pallas_call | solution.py:948
  173.1 1.7 scatter_states.4.rest_0_
  174.8 0.7 copy-done.12
  175.6 24.0 %attend.1 = (f32[4,2,128,1024]{3,2,1,0:T(8,128)}, f32[4,2,2,1024]{3,2,1,0:T(2,128)S(1)}) custom-call(s32[3]{0:T(128)S(1)} %pad_add_fusion.limits_ref, s32[16,16]{1,0:T(8,128)S(1)} %copy-done.5, s32[16]{0:T(128)S(1)} %copy-done.6, bf16[64,2,64,256]{3,2,1,0:T(8,128)(2,1)} %bitcast.62, bf16[24,2,64,256]{3,2,1,0:T(8,128)(2,1)S(1)} %copy-done.8, ...), custom_call_target="tpu_custom_call" | custom-call | flops 5368709120 | bytes 16777216 | tf_op jit(solution)/shard_map/attend/pallas_call | solution.py:988
  199.6 1.8 scatter_states.5.rest_0_
  201.4 30.1 %collective-permute-done.3.passed_ref = bf16[8,2,64,256]{3,2,1,0:T(8,128)(2,1)S(1)} collective-permute-done((bf16[8,2,64,256]{3,2,1,0:T(8,128)(2,1)}, bf16[8,2,64,256]{3,2,1,0:T(8,128)(2,1)S(1)}, u32[]{:S(2)}, u32[]{:S(2)}) %collective-permute-start.3) | collective-permute-done | bytes 524320 | tf_op jit(solution)/shard_map/ppermute | solution.py:345
  231.5 7.3 %attend_passed.1 = bf16[4,2,4,256,128]{4,3,2,1,0:T(8,128)(2,1)S(1)} custom-call(s32[3]{0:T(128)S(1)} %pad_add_fusion.limits_ref, s32[16,16]{1,0:T(8,128)S(1)} %copy-done.5, s32[16]{0:T(128)S(1)} %copy-done.6, bf16[8,2,64,256]{3,2,1,0:T(8,128)(2,1)S(1)} %collective-permute-done.3.passed_ref, bf16[4,2,4,256,128]{4,3,2,1,0:T(8,128)(2,1)S(1)} %bitcast.66, ...), custom_call_target="tpu_custom_call" | custom-call | flops 536870912 | bytes 8388608 | tf_op jit(solution)/shard_map/attend_passed/pallas_call | solution.py:1025
  238.9 0.2 copy.113
  239.1 2.7 %copy.114 = bf16[1024,8,128]{2,1,0:T(8,128)(2,1)} copy(bf16[1024,8,128]{2,0,1:T(8,128)(2,1)S(1)} %bitcast.81) | data formatting | bytes 4194304
  241.8 1.8 scatter_states.6.rest_0_
  243.5 1.7 scatter_states.7
  (98 shorter events, 2.4 us)
Async XLA Ops:
  0.7 5.0 %copy-start.18 = (s32[16,16]{1,0:T(8,128)S(1)}, s32[16,16]{1,0:T(8,128)}, u32[]{:S(2)}) copy-start(s32[16,16]{1,0:T(8,128)} %place_ref.14) | copy-start | bytes 3076
  4.0 84.9 %collective-permute-start = (bf16[16,32,4,256]{3,2,1,0:T(4,128)(2,1)}, bf16[16,32,4,256]{3,2,1,0:T(4,128)(2,1)}, u32[]{:S(2)}, u32[]{:S(2)}) collective-permute-start(bf16[16,32,4,256]{3,2,1,0:T(4,128)(2,1)} %gather_states.3), channel_id=1, source_target_pairs={{0,4},{4,8},{8,12},{12,0},{1,5},{5,9},{9,13},{13,1},{2,6},{6,10},{... | collective-permute-start | bytes 3145736 | tf_op jit(solution)/shard_map/ppermute | solution.py:786
  8.7 80.2 %collective-permute-start.1 = (bf16[16,32,4,256]{3,2,1,0:T(4,128)(2,1)}, bf16[16,32,4,256]{3,2,1,0:T(4,128)(2,1)}, u32[]{:S(2)}, u32[]{:S(2)}) collective-permute-start(bf16[16,32,4,256]{3,2,1,0:T(4,128)(2,1)} %gather_states.4), channel_id=1, source_target_pairs={{0,8},{4,12},{8,0},{12,4},{1,9},{5,13},{9,1},{13,5},{2,10},{6,14},... | collective-permute-start | bytes 3145736 | tf_op jit(solution)/shard_map/ppermute | solution.py:786
  11.4 4.4 %copy-start.19 = (bf16[1024,32]{0,1:T(8,128)(2,1)S(1)}, bf16[1024,32]{0,1:T(8,128)(2,1)}, u32[]{:S(2)}) copy-start(bf16[1024,32]{0,1:T(8,128)(2,1)} %param.27) | copy-start | bytes 196612
  11.4 4.6 %copy-start.27 = (f32[32]{0:T(128)S(1)}, f32[32]{0:T(128)}, u32[]{:S(2)}) copy-start(f32[32]{0:T(128)} %param.32) | copy-start | bytes 388
  11.4 7.5 %copy-start.5 = (s32[16,16]{1,0:T(8,128)S(1)}, s32[16,16]{1,0:T(8,128)}, u32[]{:S(2)}) copy-start(s32[16,16]{1,0:T(8,128)} %place_ref.19) | copy-start | bytes 3076
  11.4 7.7 %copy-start.6 = (s32[16]{0:T(128)S(1)}, s32[16]{0:T(128)}, u32[]{:S(2)}) copy-start(s32[16]{0:T(128)} %prefix_ref.7) | copy-start | bytes 196
  11.4 8.6 %copy-start.25 = (s32[7]{0:T(128)S(1)}, s32[7]{0:T(128)}, u32[]{:S(2)}) copy-start(s32[7]{0:T(128)} %constant.123) | copy-start | bytes 88
  11.5 9.3 %copy-start.26 = (s32[7]{0:T(128)S(1)}, s32[7]{0:T(128)}, u32[]{:S(2)}) copy-start(s32[7]{0:T(128)} %constant.122) | copy-start | bytes 88
  11.5 10.6 %copy-start.28 = (s32[7]{0:T(128)S(1)}, s32[7]{0:T(128)}, u32[]{:S(2)}) copy-start(s32[7]{0:T(128)} %constant.111.clone) | copy-start | bytes 88
  14.5 74.4 %collective-permute-start.2 = (bf16[16,32,4,256]{3,2,1,0:T(4,128)(2,1)}, bf16[16,32,4,256]{3,2,1,0:T(4,128)(2,1)}, u32[]{:S(2)}, u32[]{:S(2)}) collective-permute-start(bf16[16,32,4,256]{3,2,1,0:T(4,128)(2,1)} %gather_states.5), channel_id=1, source_target_pairs={{0,12},{4,0},{8,4},{12,8},{1,13},{5,1},{9,5},{13,9},{2,14},{6,2},{... | collective-permute-start | bytes 3145736 | tf_op jit(solution)/shard_map/ppermute | solution.py:786
  28.2 5.3 %copy-start.20 = (bf16[4,3,2048]{2,0,1:T(4,128)(2,1)S(1)}, bf16[4,3,2048]{2,0,1:T(4,128)(2,1)}, u32[]{:S(2)}) copy-start(bf16[4,3,2048]{2,0,1:T(4,128)(2,1)} %param.28) | copy-start | bytes 147460
  28.2 5.9 %copy-start.22 = (bf16[4,2048]{1,0:T(4,128)(2,1)S(1)}, bf16[4,2048]{1,0:T(4,128)(2,1)}, u32[]{:S(2)}) copy-start(bf16[4,2048]{1,0:T(4,128)(2,1)} %param.30) | copy-start | bytes 49156
  28.2 6.0 %copy-start.15 = (bf16[1024,2,512]{2,1,0:T(2,128)(2,1)S(1)}, bf16[1024,2,512]{2,1,0:T(2,128)(2,1)}, u32[]{:S(2)}) copy-start(bf16[1024,2,512]{2,1,0:T(2,128)(2,1)} %param.26) | copy-start | bytes 6291460
  33.5 1.1 copy-start.21
  34.2 1.7 copy-start.24
  36.0 12.8 %copy-start.23 = (bf16[4,2,512]{2,1,0:T(2,128)(2,1)S(1)}, bf16[4,2,512]{2,1,0:T(2,128)(2,1)}, u32[]{:S(2)}) copy-start(bf16[4,2,512]{2,1,0:T(2,128)(2,1)} %param.31) | copy-start | bytes 24580
  37.9 2.2 copy-start
  40.1 9.7 %copy-start.13 = (f32[2,16,4,256]{1,3,0,2:T(8,128)S(1)}, f32[2,16,4,256]{1,3,0,2:T(8,128)}, u32[]{:S(2)}) copy-start(f32[2,16,4,256]{1,3,0,2:T(8,128)} %copy.107) | copy-start | bytes 393220
  40.1 9.7 %copy-start.14 = (f32[2,16,4,256]{1,3,0,2:T(8,128)S(1)}, f32[2,16,4,256]{1,3,0,2:T(8,128)}, u32[]{:S(2)}) copy-start(f32[2,16,4,256]{1,3,0,2:T(8,128)} %copy.106) | copy-start | bytes 393220
  48.8 1.3 copy-start.4
  50.1 38.8 %copy-start.17 = (s32[16,16]{1,0:T(8,128)S(1)}, s32[16,16]{1,0:T(8,128)}, u32[]{:S(2)}) copy-start(s32[16,16]{1,0:T(8,128)} %place_ref.21) | copy-start | bytes 3076
  87.9 1.0 copy-start.2
  88.9 59.8 %all-to-all-start.2 = ((bf16[32,2,64,256]{3,2,1,0:T(8,128)(2,1)}), bf16[32,2,64,256]{3,2,1,0:T(8,128)(2,1)S(1)}, u32[]{:S(2)}, u32[]{:S(2)}) async-start(bf16[32,2,64,256]{3,2,1,0:T(8,128)(2,1)} %get-tuple-element.184), calls=%async_computation.2 | async-start | bytes 4194304 | tf_op jit(solution)/shard_map/cond/branch_2_fun/all_to_all | solution.py:780
  148.8 1.3 copy-start.9
  150.1 49.5 %collective-permute-start.4 = (bf16[16,32,4,256]{3,2,1,0:T(4,128)(2,1)}, bf16[16,32,4,256]{3,2,1,0:T(4,128)(2,1)S(1)}, u32[]{:S(2)}, u32[]{:S(2)}) collective-permute-start(bf16[16,32,4,256]{3,2,1,0:T(4,128)(2,1)} %get-tuple-element.366), channel_id=1, source_target_pairs={{0,4},{4,8},{8,12},{12,0},{1,5},{5,9},{9,13},{13,1},{2,6},{6,10},{... | collective-permute-start | bytes 3145736 | tf_op jit(solution)/shard_map/ppermute | solution.py:786
  150.1 91.6 %collective-permute-start.6 = (bf16[16,32,4,256]{3,2,1,0:T(4,128)(2,1)}, bf16[16,32,4,256]{3,2,1,0:T(4,128)(2,1)S(1)}, u32[]{:S(2)}, u32[]{:S(2)}) collective-permute-start(bf16[16,32,4,256]{3,2,1,0:T(4,128)(2,1)} %get-tuple-element.372), channel_id=1, source_target_pairs={{0,8},{4,12},{8,0},{12,4},{1,9},{5,13},{9,1},{13,5},{2,10},{6,14},... | collective-permute-start | bytes 3145736 | tf_op jit(solution)/shard_map/ppermute | solution.py:786
  153.0 90.5 %collective-permute-start.5 = (bf16[16,32,4,256]{3,2,1,0:T(4,128)(2,1)}, bf16[16,32,4,256]{3,2,1,0:T(4,128)(2,1)S(1)}, u32[]{:S(2)}, u32[]{:S(2)}) collective-permute-start(bf16[16,32,4,256]{3,2,1,0:T(4,128)(2,1)} %get-tuple-element.371), channel_id=1, source_target_pairs={{0,12},{4,0},{8,4},{12,8},{1,13},{5,1},{9,5},{13,9},{2,14},{6,2},{... | collective-permute-start | bytes 3145736 | tf_op jit(solution)/shard_map/ppermute | solution.py:786
  153.9 3.8 %copy-start.1 = (bf16[64,64,2,256]{3,1,2,0:T(8,128)(2,1)S(1)}, bf16[64,64,2,256]{3,1,2,0:T(8,128)(2,1)}, u32[]{:S(2)}) copy-start(bf16[64,64,2,256]{3,1,2,0:T(8,128)(2,1)} %copy.129) | copy-start | bytes 12582916
  153.9 3.8 %copy-start.8 = (bf16[24,2,64,256]{3,2,1,0:T(8,128)(2,1)S(1)}, bf16[24,2,64,256]{3,2,1,0:T(8,128)(2,1)}, u32[]{:S(2)}) copy-start(bf16[24,2,64,256]{3,2,1,0:T(8,128)(2,1)} %get-tuple-element.359.rest_0_) | copy-start | bytes 4718596
  157.8 4.5 %copy-start.3 = (bf16[2,1024,256]{2,1,0:T(8,128)(2,1)S(1)}, bf16[2,1024,256]{2,1,0:T(8,128)(2,1)}, u32[]{:S(2)}) copy-start(bf16[2,1024,256]{2,1,0:T(8,128)(2,1)} %copy-done.2) | copy-start | bytes 3145732
  161.3 70.2 %collective-permute-start.3 = (bf16[8,2,64,256]{3,2,1,0:T(8,128)(2,1)}, bf16[8,2,64,256]{3,2,1,0:T(8,128)(2,1)S(1)}, u32[]{:S(2)}, u32[]{:S(2)}) collective-permute-start(bf16[8,2,64,256]{3,2,1,0:T(8,128)(2,1)} %pass_pages_on.1), channel_id=1, source_target_pairs={{0,4},{4,0},{8,12},{12,8},{1,5},{5,1},{9,13},{13,9},{2,6},{6,2},{1... | collective-permute-start | bytes 1572872 | tf_op jit(solution)/shard_map/ppermute | solution.py:345
  162.3 10.8 %copy-start.16 = (bf16[16,32,4,256]{3,2,1,0:T(4,128)(2,1)S(1)}, bf16[16,32,4,256]{3,2,1,0:T(4,128)(2,1)}, u32[]{:S(2)}) copy-start(bf16[16,32,4,256]{3,2,1,0:T(4,128)(2,1)} %get-tuple-element.367.got_ref) | copy-start | bytes 3145732
  173.1 1.7 copy-start.10
  173.1 2.5 %copy-start.12 = (bf16[28,2,64,256]{3,2,1,0:T(8,128)(2,1)S(1)}, bf16[28,2,64,256]{3,2,1,0:T(8,128)(2,1)}, u32[]{:S(2)}) copy-start(bf16[28,2,64,256]{3,2,1,0:T(8,128)(2,1)} %get-tuple-element.360.rest_1_) | copy-start | bytes 5505028
